TPU v7x, 32 devices: a whole 2x2x4 slice. The times are simulated.
32 devices in a mesh: ctx: 8 (over y, x, core), tp: 4 (over z).
Axes of the slice: x: 2, y: 2, z: 4, core: 2. Of those that a mesh axis runs over, the one named last changes fastest.
Arguments:
- hyena_gate: bfloat16 [1024, 4096], P('ctx', 'tp'), may hold values from -6 to 6
- hyena_key: bfloat16 [1024, 4096], P('ctx', 'tp'), may hold values from -6 to 6
- hyena_value: bfloat16 [1024, 4096], P('ctx', 'tp'), may hold values from -6 to 6
- filter_taps: bfloat16 [1024, 4096], P(None, 'tp'), may hold values from -0.25 to 0.25
- skip_weight: float32 [4096], P('tp'), may hold values from -4 to 4
- queries: bfloat16 [1024, 4096], P('ctx', 'tp'), may hold values from -100 to 100
- attn_keys: bfloat16 [1024, 4096], P('ctx', 'tp'), may hold values from -4.5 to 4.5
- valid_length: int32 [1], replicated, may hold values from 513 to 1024
Outputs:
- hyena_out: bfloat16 [1024, 4096], P('ctx', 'tp')
- attn_out: bfloat16 [1024, 4096], P('ctx', 'tp')
All inputs are finite; a program needn't handle non-finite values.
Results may differ from a plain program's by a relative error of at most 0.015.
Values may be sent and summed in bfloat16 or wider, within the bound.
A program may use at most 64 MiB of HBM per device.

v0:
```python
import functools
import math

import jax
import jax.numpy as jnp
import numpy as np
from jax import lax
from jax.experimental import pallas as pl
from jax.experimental.pallas import tpu as pltpu
from jax.sharding import PartitionSpec as P

HD = 128
DW = 4096


def tables(group_rows):
    doubled = 2 * group_rows
    freq = jnp.arange(doubled, dtype=jnp.int32)[:, None]
    place = jnp.arange(group_rows, dtype=jnp.int32)[None, :]
    phase = (freq * place % doubled).astype(jnp.float32) * (2.0 * math.pi / doubled)
    parity = (1 - 2 * (jnp.arange(doubled, dtype=jnp.int32) % 2)).astype(jnp.float32)[:, None]
    cosine = jnp.cos(phase)
    sine = jnp.sin(phase)
    cos_high = cosine.astype(jnp.bfloat16)
    cos_low = (cosine - cos_high.astype(jnp.float32)).astype(jnp.bfloat16)
    sin_high = sine.astype(jnp.bfloat16)
    sin_low = (sine - sin_high.astype(jnp.float32)).astype(jnp.bfloat16)
    return ((cos_high, cos_low, sin_high, sin_low, cosine, sine), parity)


def split_dot(high, low, block):
    return jnp.dot(high, block, preferred_element_type=jnp.float32) + jnp.dot(
        low, block, preferred_element_type=jnp.float32
    )


def forward(tabs, block):
    return (split_dot(tabs[0], tabs[1], block), -split_dot(tabs[2], tabs[3], block))


def inverse(tabs, real_part, imag_part):
    cosine, sine = (tabs[4], tabs[5])
    scale = 1.0 / cosine.shape[0]
    first = jnp.dot(
        cosine.T, real_part, precision=lax.Precision.HIGH, preferred_element_type=jnp.float32
    )
    second = jnp.dot(
        sine.T, imag_part, precision=lax.Precision.HIGH, preferred_element_type=jnp.float32
    )
    return (first - second) * scale


def complex_mul(left_real, left_imag, right_real, right_imag):
    return (
        left_real * right_real - left_imag * right_imag,
        left_real * right_imag + left_imag * right_real,
    )


def shards(
    hyena_gate, hyena_key, hyena_value, filter_taps, skip_weight, queries, attn_keys, valid_length
):
    group_rows = hyena_gate.shape[0]
    ranks = lax.axis_size("ctx")
    own_index = lax.axis_index("ctx")
    tabs, parity = tables(group_rows)
    mixed = (hyena_key.astype(jnp.float32) * hyena_value.astype(jnp.float32)).astype(jnp.bfloat16)
    mixed_float = mixed.astype(jnp.float32)
    input_real, input_imag = forward(tabs, mixed)
    own_block = lax.dynamic_slice_in_dim(filter_taps, own_index * group_rows, group_rows, 0)
    taps_real, taps_imag = forward(tabs, own_block)
    band = 2 * group_rows // ranks
    in_real = lax.all_to_all(
        input_real[None].astype(jnp.bfloat16), "ctx", split_axis=1, concat_axis=0, tiled=True
    ).astype(jnp.float32)
    in_imag = lax.all_to_all(
        input_imag[None].astype(jnp.bfloat16), "ctx", split_axis=1, concat_axis=0, tiled=True
    ).astype(jnp.float32)
    filt_real = lax.all_to_all(
        taps_real[None].astype(jnp.bfloat16), "ctx", split_axis=1, concat_axis=0, tiled=True
    ).astype(jnp.float32)
    filt_imag = lax.all_to_all(
        taps_imag[None].astype(jnp.bfloat16), "ctx", split_axis=1, concat_axis=0, tiled=True
    ).astype(jnp.float32)
    band_parity = lax.dynamic_slice_in_dim(parity, own_index * band, band, 0)[None]
    prior_real = jnp.concatenate([jnp.zeros_like(filt_real[:1]), filt_real[:-1]], 0)
    prior_imag = jnp.concatenate([jnp.zeros_like(filt_imag[:1]), filt_imag[:-1]], 0)
    lag_real = filt_real + band_parity * prior_real
    lag_imag = filt_imag + band_parity * prior_imag
    order = jnp.arange(ranks, dtype=jnp.int32)[:, None, None]

    def add_lag(lag, inner):
        later = order >= lag
        moved_real = jnp.where(later, jnp.roll(in_real, lag, 0), 0.0)
        moved_imag = jnp.where(later, jnp.roll(in_imag, lag, 0), 0.0)
        this_real = lax.dynamic_index_in_dim(lag_real, lag, 0, keepdims=True)
        this_imag = lax.dynamic_index_in_dim(lag_imag, lag, 0, keepdims=True)
        out_real, out_imag = complex_mul(this_real, this_imag, moved_real, moved_imag)
        return (inner[0] + out_real, inner[1] + out_imag)

    zeros = jnp.zeros_like(in_real)
    sum_real, sum_imag = lax.fori_loop(0, ranks, add_lag, (zeros, zeros))
    total_real = lax.all_to_all(
        sum_real.astype(jnp.bfloat16), "ctx", split_axis=0, concat_axis=1, tiled=True
    ).astype(sum_real.dtype)
    total_imag = lax.all_to_all(
        sum_imag.astype(jnp.bfloat16), "ctx", split_axis=0, concat_axis=1, tiled=True
    ).astype(sum_imag.dtype)
    convolved = inverse(tabs, total_real[0], total_imag[0])
    positions = own_index * group_rows + jnp.arange(group_rows, dtype=jnp.int32)
    valid_rows = (positions < valid_length[0])[:, None]
    gated = hyena_gate.astype(jnp.float32) * (convolved + skip_weight[None, :] * mixed_float)
    hyena_out = jnp.where(valid_rows, gated, 0.0).astype(jnp.bfloat16)
    heads_here = queries.shape[1] // HD
    scale = 1.0 / math.sqrt(HD)
    query_heads = queries.reshape(group_rows, heads_here, HD)
    start_max = jnp.full((heads_here, group_rows), -1e30, jnp.float32)
    key_piece = lax.all_gather(attn_keys, "ctx", axis=0, tiled=True)
    value_piece = lax.all_gather(hyena_out, "ctx", axis=0, tiled=True)
    width = key_piece.shape[0]
    key_heads = key_piece.reshape(width, heads_here, HD)
    value_heads = value_piece.reshape(width, heads_here, HD)
    scores = (
        jnp.einsum("qhd,khd->hqk", query_heads, key_heads, preferred_element_type=jnp.float32)
        * scale
    )
    key_places = jnp.arange(width, dtype=jnp.int32)
    allowed = (key_places[None, :] <= positions[:, None]) & (key_places < valid_length[0])[None, :]
    scores = jnp.where(allowed[None], scores, -1e30)
    new_max = jnp.maximum(start_max, jnp.max(scores, axis=2))
    weights = jnp.where(allowed[None], jnp.exp(scores - new_max[:, :, None]), 0.0)
    totals = jnp.sum(weights, axis=2)
    update = jnp.einsum(
        "hqk,khd->hqd",
        weights.astype(jnp.bfloat16),
        value_heads,
        preferred_element_type=jnp.float32,
    )
    attended = (update / totals[:, :, None]).transpose(1, 0, 2).reshape(group_rows, heads_here * HD)
    squares = jnp.sum(attended * attended, axis=1)
    total_squares = lax.psum(squares, "tp")
    scaled = attended / jnp.sqrt(total_squares / DW + 1e-06)[:, None]
    attn_out = jnp.where(valid_rows, scaled, 0.0).astype(jnp.bfloat16)
    return (hyena_out, attn_out)


MESH = pl.DeviceIdType.MESH
MIX, GATE, KEY, QUERY = range(4)


def half_shift_tables(block):
    freq = np.arange(block, dtype=np.float64)[:, None] + 0.5
    place = np.arange(2 * block, dtype=np.float64)[None, :] - block
    phase = freq * place * (math.pi / block)
    ahead = np.concatenate([np.cos(phase), -np.sin(phase)], 0)
    back = ahead[:, block:].T / block

    def split(table):
        high = table.astype(jnp.bfloat16)
        low = (table - high.astype(np.float64)).astype(jnp.bfloat16)
        return high, low

    return split(ahead) + split(back)


def head_kernel(
    ranks,
    depth,
    hk,
    hv,
    gate,
    taps,
    skip,
    queries,
    keys,
    valid,
    ahead_high,
    ahead_low,
    back_high,
    back_low,
    h_out,
    a_out,
    hk_v,
    hv_v,
    mix_v,
    taps_v,
    ah_v,
    al_v,
    bh_v,
    bl_v,
    got,
    lag_s,
    in_s,
    sum_high,
    sum_low,
    h_buf,
    a_buf,
    a_in,
    sq_mine,
    sq_in,
    local_sem,
    in_send,
    in_recv,
    h_send,
    h_recv,
    a_send,
    a_recv,
    sq_send,
    sq_recv,
):
    me = lax.axis_index("ctx")
    plane = lax.axis_index("tp")
    group = hk_v.shape[0]
    seq = ranks * group
    block = bh_v.shape[0]
    blocks = seq // block
    per_block = block // group

    def columns(index):
        return pl.ds(pl.multiple_of(index * HD, HD), HD)

    own = columns(me)
    local = [
        pltpu.make_async_copy(src, dst, local_sem.at[i])
        for i, (src, dst) in enumerate(
            (
                (hk, hk_v),
                (hv, hv_v),
                (taps.at[:, own], taps_v.at[pl.ds(block, seq)]),
                (ahead_high, ah_v),
                (ahead_low, al_v),
                (back_high, bh_v),
                (back_low, bl_v),
                (gate.at[:, own], got.at[GATE, me]),
                (keys.at[:, own], got.at[KEY, me]),
                (queries.at[:, own], got.at[QUERY, me]),
            )
        )
    ]
    for copy in local:
        copy.start()

    barrier = pltpu.get_barrier_semaphore()
    for step in range(1, ranks):
        pl.semaphore_signal(
            barrier, inc=1, device_id={"ctx": lax.rem(me + step, ranks)}, device_id_type=MESH
        )
    for step in range(1, depth):
        pl.semaphore_signal(
            barrier, inc=1, device_id={"tp": lax.rem(plane + step, depth)}, device_id_type=MESH
        )
    local[0].wait()
    local[1].wait()
    mix_v[...] = (hk_v[...].astype(jnp.float32) * hv_v[...].astype(jnp.float32)).astype(
        jnp.bfloat16
    )
    pl.semaphore_wait(barrier, ranks - 1 + depth - 1)

    sends = []
    for which, src in ((MIX, mix_v), (GATE, gate), (KEY, keys), (QUERY, queries)):
        for step in range(1, ranks):
            peer = lax.rem(me + step, ranks)
            copy = pltpu.make_async_remote_copy(
                src_ref=src.at[:, columns(peer)],
                dst_ref=got.at[which, me],
                send_sem=in_send.at[which, step],
                recv_sem=in_recv.at[which, me],
                device_id={"ctx": peer},
                device_id_type=MESH,
            )
            copy.start()
            sends.append(copy)

    def arrive(which):
        for step in range(1, ranks):
            peer = lax.rem(me + step, ranks)
            pltpu.make_async_remote_copy(
                src_ref=got.at[which, peer],
                dst_ref=got.at[which, peer],
                send_sem=in_send.at[which, step],
                recv_sem=in_recv.at[which, peer],
                device_id={"ctx": peer},
                device_id_type=MESH,
            ).wait_recv()

    got[MIX, me] = mix_v[:, own]
    taps_v[:block] = jnp.zeros((block, HD), jnp.bfloat16)
    for copy in local[2:7]:
        copy.wait()
    windows = jnp.concatenate(
        [taps_v[i * block : (i + 2) * block] for i in range(blocks)], axis=1
    )
    lag_s[...] = jnp.dot(ah_v[...], windows, preferred_element_type=jnp.float32) + jnp.dot(
        al_v[...], windows, preferred_element_type=jnp.float32
    )

    arrive(MIX)
    mixed = got[MIX].reshape(seq, HD)
    inputs = jnp.concatenate([mixed[i * block : (i + 1) * block] for i in range(blocks)], axis=1)
    in_s[...] = jnp.dot(
        ah_v[:, block:], inputs, preferred_element_type=jnp.float32
    ) + jnp.dot(al_v[:, block:], inputs, preferred_element_type=jnp.float32)

    rows_at_once = 16

    def multiply(step, carry):
        first = pl.multiple_of(step * rows_at_once, rows_at_once)
        real_rows = pl.ds(first, rows_at_once)
        imag_rows = pl.ds(block + first, rows_at_once)
        lanes = [slice(i * HD, (i + 1) * HD) for i in range(blocks)]
        in_real = [in_s[real_rows, s] for s in lanes]
        in_imag = [in_s[imag_rows, s] for s in lanes]
        lag_real = [lag_s[real_rows, s] for s in lanes]
        lag_imag = [lag_s[imag_rows, s] for s in lanes]
        for i in range(blocks):
            real = imag = None
            for j in range(i + 1):
                a, b, c, d = lag_real[i - j], lag_imag[i - j], in_real[j], in_imag[j]
                more_real = a * c - b * d
                more_imag = a * d + b * c
                real = more_real if real is None else real + more_real
                imag = more_imag if imag is None else imag + more_imag
            for rows, total in ((real_rows, real), (imag_rows, imag)):
                high = total.astype(jnp.bfloat16)
                sum_high[rows, lanes[i]] = high
                sum_low[rows, lanes[i]] = (total - high.astype(jnp.float32)).astype(jnp.bfloat16)
        return carry

    lax.fori_loop(0, block // rows_at_once, multiply, 0)
    convolved = (
        jnp.dot(bh_v[...], sum_high[...], preferred_element_type=jnp.float32)
        + jnp.dot(bl_v[...], sum_high[...], preferred_element_type=jnp.float32)
        + jnp.dot(bh_v[...], sum_low[...], preferred_element_type=jnp.float32)
    )

    length = valid[0]
    weight = skip[:, own]
    local[7].wait()
    arrive(GATE)
    row_ids = lax.broadcasted_iota(jnp.int32, (group, HD), 0)
    lane_ids = lax.broadcasted_iota(jnp.int32, (group, HD), 1)
    for g in range(ranks):
        part = convolved[
            g % per_block * group : (g % per_block + 1) * group,
            g // per_block * HD : (g // per_block + 1) * HD,
        ]
        gated = got[GATE, g].astype(jnp.float32) * (
            part + weight * got[MIX, g].astype(jnp.float32)
        )
        h_buf[g] = jnp.where(row_ids + g * group < length, gated, 0.0).astype(jnp.bfloat16)

    h_local = pltpu.make_async_copy(h_buf.at[me], h_out.at[:, own], local_sem.at[0])
    h_local.start()
    for step in range(1, ranks):
        peer = lax.rem(me + step, ranks)
        copy = pltpu.make_async_remote_copy(
            src_ref=h_buf.at[peer],
            dst_ref=h_out.at[:, own],
            send_sem=h_send.at[step],
            recv_sem=h_recv.at[me],
            device_id={"ctx": peer},
            device_id_type=MESH,
        )
        copy.start()
        sends.append(copy)

    local[8].wait()
    local[9].wait()
    arrive(KEY)
    arrive(QUERY)
    factor = math.log2(math.e) / math.sqrt(HD)
    order = [g for low in range(per_block - 1, -1, -1) for g in range(ranks - per_block + low, -1, -per_block)]

    def attended_copy(g, source):
        return pltpu.make_async_remote_copy(
            src_ref=a_buf.at[g],
            dst_ref=a_in.at[source],
            send_sem=a_send.at[g],
            recv_sem=a_recv.at[source],
            device_id={"ctx": g},
            device_id_type=MESH,
        )

    for g in order:
        width = (g + 1) * group
        score = lax.dot_general(
            got[QUERY, g],
            got[KEY, : g + 1].reshape(width, HD),
            (((1,), (1,)), ((), ())),
            preferred_element_type=jnp.float32,
        )
        last = jnp.where(lane_ids <= row_ids, score[:, g * group :], -1e30)
        score = last if g == 0 else jnp.concatenate([score[:, : g * group], last], axis=1)
        row_max = jnp.max(score, axis=1, keepdims=True)
        raw = jnp.exp2((score - row_max) * factor)
        totals = jnp.sum(raw, axis=1, keepdims=True)
        update = jnp.dot(
            raw.astype(jnp.bfloat16),
            h_buf[: g + 1].reshape(width, HD),
            preferred_element_type=jnp.float32,
        )
        a_buf[g] = (update / totals).astype(jnp.bfloat16)

        @pl.when(me != g)
        def _():
            attended_copy(g, me).start()

    a_in[me] = a_buf[me]
    for step in range(1, ranks):
        peer = lax.rem(me + step, ranks)
        attended_copy(peer, peer).wait_recv()

    squares = jnp.zeros((group, HD), jnp.float32)
    for s in range(ranks):
        piece = a_in[s].astype(jnp.float32)
        squares = squares + piece * piece
    row_squares = jnp.sum(squares.T, axis=0, keepdims=True)
    sq_mine[...] = jnp.broadcast_to(row_squares, sq_mine.shape)
    for step in range(1, depth):
        other = lax.rem(plane + step, depth)
        copy = pltpu.make_async_remote_copy(
            src_ref=sq_mine,
            dst_ref=sq_in.at[plane],
            send_sem=sq_send.at[step],
            recv_sem=sq_recv.at[plane],
            device_id={"tp": other},
            device_id_type=MESH,
        )
        copy.start()
        sends.append(copy)
    total_squares = sq_mine[:1]
    for step in range(1, depth):
        other = lax.rem(plane + step, depth)
        pltpu.make_async_remote_copy(
            src_ref=sq_in.at[other],
            dst_ref=sq_in.at[other],
            send_sem=sq_send.at[step],
            recv_sem=sq_recv.at[other],
            device_id={"tp": other},
            device_id_type=MESH,
        ).wait_recv()
        total_squares = total_squares + sq_in[other][:1]
    inverse_norm = lax.rsqrt(total_squares * (1.0 / (depth * ranks * HD)) + 1e-06)
    by_row = jnp.broadcast_to(inverse_norm, (group, HD)).T
    by_row = jnp.where(row_ids + me * group < length, by_row, 0.0)
    for s in range(ranks):
        a_out[:, s * HD : (s + 1) * HD] = (a_in[s].astype(jnp.float32) * by_row).astype(
            jnp.bfloat16
        )

    h_local.wait()
    for step in range(1, ranks):
        peer = lax.rem(me + step, ranks)
        pltpu.make_async_remote_copy(
            src_ref=h_buf.at[peer],
            dst_ref=h_out.at[:, columns(peer)],
            send_sem=h_send.at[step],
            recv_sem=h_recv.at[peer],
            device_id={"ctx": peer},
            device_id_type=MESH,
        ).wait_recv()
        attended_copy(peer, me).wait_send()
    for copy in sends:
        copy.wait_send()


def head_shards(ranks, depth, *arrays):
    hyena_gate, hyena_key, hyena_value, filter_taps, skip_weight, queries, attn_keys, valid = arrays
    group, channels = hyena_gate.shape
    seq = filter_taps.shape[0]
    block = 2 * group if ranks % 2 == 0 else group
    blocks = seq // block
    bf16, f32 = jnp.bfloat16, jnp.float32
    any_space = pl.BlockSpec(memory_space=pl.ANY)
    vmem = pl.BlockSpec(memory_space=pltpu.VMEM)
    smem = pl.BlockSpec(memory_space=pltpu.SMEM)
    return pl.pallas_call(
        functools.partial(head_kernel, ranks, depth),
        out_shape=(
            jax.ShapeDtypeStruct((group, channels), bf16),
            jax.ShapeDtypeStruct((group, channels), bf16),
        ),
        in_specs=[any_space] * 4 + [vmem] + [any_space] * 2 + [smem] + [any_space] * 4,
        out_specs=(any_space, vmem),
        scratch_shapes=[
            pltpu.VMEM((group, channels), bf16),
            pltpu.VMEM((group, channels), bf16),
            pltpu.VMEM((group, channels), bf16),
            pltpu.VMEM((block + seq, HD), bf16),
            pltpu.VMEM((2 * block, 2 * block), bf16),
            pltpu.VMEM((2 * block, 2 * block), bf16),
            pltpu.VMEM((block, 2 * block), bf16),
            pltpu.VMEM((block, 2 * block), bf16),
            pltpu.VMEM((4, ranks, group, HD), bf16),
            pltpu.VMEM((2 * block, blocks * HD), f32),
            pltpu.VMEM((2 * block, blocks * HD), f32),
            pltpu.VMEM((2 * block, blocks * HD), bf16),
            pltpu.VMEM((2 * block, blocks * HD), bf16),
            pltpu.VMEM((ranks, group, HD), bf16),
            pltpu.VMEM((ranks, group, HD), bf16),
            pltpu.VMEM((ranks, group, HD), bf16),
            pltpu.VMEM((8, group), f32),
            pltpu.VMEM((depth, 8, group), f32),
            pltpu.SemaphoreType.DMA((10,)),
            pltpu.SemaphoreType.DMA((4, ranks)),
            pltpu.SemaphoreType.DMA((4, ranks)),
            pltpu.SemaphoreType.DMA((ranks,)),
            pltpu.SemaphoreType.DMA((ranks,)),
            pltpu.SemaphoreType.DMA((ranks,)),
            pltpu.SemaphoreType.DMA((ranks,)),
            pltpu.SemaphoreType.DMA((depth,)),
            pltpu.SemaphoreType.DMA((depth,)),
        ],
        compiler_params=pltpu.CompilerParams(
            collective_id=0, has_side_effects=True, vmem_limit_bytes=40 * 1024 * 1024
        ),
    )(
        hyena_key,
        hyena_value,
        hyena_gate,
        filter_taps,
        skip_weight.reshape(1, channels),
        queries,
        attn_keys,
        valid,
        *(jnp.asarray(table) for table in half_shift_tables(block)),
    )


def solution(mesh):
    in_specs = (
        P("ctx", "tp"),
        P("ctx", "tp"),
        P("ctx", "tp"),
        P(None, "tp"),
        P("tp"),
        P("ctx", "tp"),
        P("ctx", "tp"),
        P(),
    )
    out_specs = (P("ctx", "tp"), P("ctx", "tp"))
    ranks, depth = mesh.shape["ctx"], mesh.shape["tp"]
    body = functools.partial(head_shards, ranks, depth) if DW // depth == ranks * HD else shards
    return jax.shard_map(
        body, mesh=mesh, in_specs=in_specs, out_specs=out_specs, check_vma=False
    )
```

profile of v0, /device:TPU:0, one launch (start us, length us, event | category | flops | bytes accessed | tf_op | source)
XLA Modules:
  0.0 45.0 jit_solution(14496374947842225959)
XLA Ops:
  1.3 0.0 copy-start
  1.3 1.6 %copy-done = bf16[1024,1024]{1,0:T(8,128)(2,1)S(1)} copy-done((bf16[1024,1024]{1,0:T(8,128)(2,1)S(1)}, bf16[1024,1024]{1,0:T(8,128)(2,1)}, u32[]{:S(2)}) %copy-start) | copy-done | bytes 2097176
  2.9 0.0 copy-start.1
  2.9 1.0 %copy-done.1 = bf16[512,512]{1,0:T(8,128)(2,1)S(1)} copy-done((bf16[512,512]{1,0:T(8,128)(2,1)S(1)}, bf16[512,512]{1,0:T(8,128)(2,1)}, u32[]{:S(2)}) %copy-start.1) | copy-done | bytes 524312
  3.9 0.0 copy-start.2
  3.9 1.0 %copy-done.2 = bf16[512,512]{1,0:T(8,128)(2,1)S(1)} copy-done((bf16[512,512]{1,0:T(8,128)(2,1)S(1)}, bf16[512,512]{1,0:T(8,128)(2,1)}, u32[]{:S(2)}) %copy-start.2) | copy-done | bytes 524312
  5.0 0.0 copy-start.3
  5.0 0.9 %copy-done.3 = bf16[128,1024]{1,0:T(8,128)(2,1)S(1)} copy-done((bf16[128,1024]{1,0:T(8,128)(2,1)S(1)}, bf16[128,1024]{1,0:T(8,128)(2,1)}, u32[]{:S(2)}) %copy-start.3) | copy-done | bytes 262168
  5.9 0.0 copy-start.4
  5.9 0.9 %copy-done.4 = bf16[128,1024]{1,0:T(8,128)(2,1)S(1)} copy-done((bf16[128,1024]{1,0:T(8,128)(2,1)S(1)}, bf16[128,1024]{1,0:T(8,128)(2,1)}, u32[]{:S(2)}) %copy-start.4) | copy-done | bytes 262168
  6.9 0.0 copy-start.5
  6.9 0.9 %copy-done.5 = bf16[128,1024]{1,0:T(8,128)(2,1)S(1)} copy-done((bf16[128,1024]{1,0:T(8,128)(2,1)S(1)}, bf16[128,1024]{1,0:T(8,128)(2,1)}, u32[]{:S(2)}) %copy-start.5) | copy-done | bytes 262168
  7.8 0.0 copy-start.6
  7.8 0.9 %copy-done.6 = bf16[128,1024]{1,0:T(8,128)(2,1)S(1)} copy-done((bf16[128,1024]{1,0:T(8,128)(2,1)S(1)}, bf16[128,1024]{1,0:T(8,128)(2,1)}, u32[]{:S(2)}) %copy-start.6) | copy-done | bytes 262168
  8.8 0.0 copy-start.7
  8.8 0.9 %copy-done.7 = bf16[128,1024]{1,0:T(8,128)(2,1)S(1)} copy-done((bf16[128,1024]{1,0:T(8,128)(2,1)S(1)}, bf16[128,1024]{1,0:T(8,128)(2,1)}, u32[]{:S(2)}) %copy-start.7) | copy-done | bytes 262168
  9.7 0.0 copy-start.8
  9.7 0.9 %copy-done.8 = bf16[256,512]{1,0:T(8,128)(2,1)S(1)} copy-done((bf16[256,512]{1,0:T(8,128)(2,1)S(1)}, bf16[256,512]{1,0:T(8,128)(2,1)}, u32[]{:S(2)}) %copy-start.8) | copy-done | bytes 262168
  10.7 0.0 copy-start.9
  10.7 0.9 %copy-done.9 = bf16[256,512]{1,0:T(8,128)(2,1)S(1)} copy-done((bf16[256,512]{1,0:T(8,128)(2,1)S(1)}, bf16[256,512]{1,0:T(8,128)(2,1)}, u32[]{:S(2)}) %copy-start.9) | copy-done | bytes 262168
  11.6 0.0 copy-start.10
  11.6 0.7 %copy-done.10 = f32[1024]{0:T(1024)S(1)} copy-done((f32[1024]{0:T(1024)S(1)}, f32[1024]{0:T(1024)}, u32[]{:S(2)}) %copy-start.10) | copy-done | bytes 4120
  12.3 31.3 %shard_map.131 = (bf16[128,1024]{1,0:T(8,128)(2,1)S(1)}, bf16[128,1024]{1,0:T(8,128)(2,1)S(1)}) custom-call(bf16[128,1024]{1,0:T(8,128)(2,1)S(1)} %copy-done.3, bf16[128,1024]{1,0:T(8,128)(2,1)S(1)} %copy-done.4, bf16[128,1024]{1,0:T(8,128)(2,1)S(1)} %copy-done.5, bf16[1024,1024]{1,0:T(8,128)(2,1)S(1)} %copy-done, f32[1,1024]{1,0:T(1,128)S(1)} %bitcast.1, ...), custom_call_target="tpu_custom_call" | custom-call | tf_op jit(solution)/shard_map/pallas_call | solution.py:477
  43.6 0.7 %copy.17 = bf16[128,1024]{1,0:T(8,128)(2,1)} copy(bf16[128,1024]{1,0:T(8,128)(2,1)S(1)} %get-tuple-element.4) | data formatting | bytes 524288
  44.3 0.7 %copy.18 = bf16[128,1024]{1,0:T(8,128)(2,1)} copy(bf16[128,1024]{1,0:T(8,128)(2,1)S(1)} %get-tuple-element.5) | data formatting | bytes 524288
Async XLA Ops:
  1.3 1.6 %copy-start = (bf16[1024,1024]{1,0:T(8,128)(2,1)S(1)}, bf16[1024,1024]{1,0:T(8,128)(2,1)}, u32[]{:S(2)}) copy-start(bf16[1024,1024]{1,0:T(8,128)(2,1)} %taps.1) | copy-start | bytes 6291460
  2.9 1.0 %copy-start.1 = (bf16[512,512]{1,0:T(8,128)(2,1)S(1)}, bf16[512,512]{1,0:T(8,128)(2,1)}, u32[]{:S(2)}) copy-start(bf16[512,512]{1,0:T(8,128)(2,1)} %constant.9.clone.ahead_low) | copy-start | bytes 1572868
  3.9 1.0 %copy-start.2 = (bf16[512,512]{1,0:T(8,128)(2,1)S(1)}, bf16[512,512]{1,0:T(8,128)(2,1)}, u32[]{:S(2)}) copy-start(bf16[512,512]{1,0:T(8,128)(2,1)} %constant.8.clone.ahead_high) | copy-start | bytes 1572868
  5.0 0.9 %copy-start.3 = (bf16[128,1024]{1,0:T(8,128)(2,1)S(1)}, bf16[128,1024]{1,0:T(8,128)(2,1)}, u32[]{:S(2)}) copy-start(bf16[128,1024]{1,0:T(8,128)(2,1)} %hk.1) | copy-start | bytes 786436
  5.9 0.9 %copy-start.4 = (bf16[128,1024]{1,0:T(8,128)(2,1)S(1)}, bf16[128,1024]{1,0:T(8,128)(2,1)}, u32[]{:S(2)}) copy-start(bf16[128,1024]{1,0:T(8,128)(2,1)} %hv.1) | copy-start | bytes 786436
  6.9 0.9 %copy-start.5 = (bf16[128,1024]{1,0:T(8,128)(2,1)S(1)}, bf16[128,1024]{1,0:T(8,128)(2,1)}, u32[]{:S(2)}) copy-start(bf16[128,1024]{1,0:T(8,128)(2,1)} %gate.1) | copy-start | bytes 786436
  7.8 0.9 %copy-start.6 = (bf16[128,1024]{1,0:T(8,128)(2,1)S(1)}, bf16[128,1024]{1,0:T(8,128)(2,1)}, u32[]{:S(2)}) copy-start(bf16[128,1024]{1,0:T(8,128)(2,1)} %queries.1) | copy-start | bytes 786436
  8.8 0.9 %copy-start.7 = (bf16[128,1024]{1,0:T(8,128)(2,1)S(1)}, bf16[128,1024]{1,0:T(8,128)(2,1)}, u32[]{:S(2)}) copy-start(bf16[128,1024]{1,0:T(8,128)(2,1)} %keys.1) | copy-start | bytes 786436
  9.7 0.9 %copy-start.8 = (bf16[256,512]{1,0:T(8,128)(2,1)S(1)}, bf16[256,512]{1,0:T(8,128)(2,1)}, u32[]{:S(2)}) copy-start(bf16[256,512]{1,0:T(8,128)(2,1)} %constant.11.clone.back_low) | copy-start | bytes 786436
  10.7 0.9 %copy-start.9 = (bf16[256,512]{1,0:T(8,128)(2,1)S(1)}, bf16[256,512]{1,0:T(8,128)(2,1)}, u32[]{:S(2)}) copy-start(bf16[256,512]{1,0:T(8,128)(2,1)} %constant.10.clone.back_high) | copy-start | bytes 786436
  11.6 0.7 %copy-start.10 = (f32[1024]{0:T(1024)S(1)}, f32[1024]{0:T(1024)}, u32[]{:S(2)}) copy-start(f32[1024]{0:T(1024)} %param.16) | copy-start | bytes 12292
where the time goes:
time: 45.5 us; the launch traced here: 45 us
  Pallas kernels  31.3 us (69%)
  local copies, waits for them, and re-layouts  12.4 us (27%)
  between operations  1.31 us (3%)
    pallas_call x1, Pallas kernels, head_shards(): pl.pallas_call(functools.partial(head_kernel, ranks, depth), out_shape=(j...  31.3 us
    unnamed x24, local copies, waits for them, and re-layouts  12.4 us

commit v1 on v0

--- a/solution.py
+++ b/solution.py
@@ -196,8 +196,12 @@
     h_buf,
     a_buf,
     a_in,
+    skip_v,
+    length_s,
     sq_mine,
     sq_in,
+    sq_sum,
+    sq_got,
     local_sem,
     in_send,
     in_recv,
@@ -207,6 +211,8 @@
     a_recv,
     sq_send,
     sq_recv,
+    total_send,
+    total_recv,
 ):
     me = lax.axis_index("ctx")
     plane = lax.axis_index("tp")
@@ -234,6 +240,8 @@
                 (gate.at[:, own], got.at[GATE, me]),
                 (keys.at[:, own], got.at[KEY, me]),
                 (queries.at[:, own], got.at[QUERY, me]),
+                (skip.at[:, own], skip_v),
+                (valid, length_s),
             )
         )
     ]
@@ -333,9 +341,11 @@
         + jnp.dot(bh_v[...], sum_low[...], preferred_element_type=jnp.float32)
     )
 
-    length = valid[0]
-    weight = skip[:, own]
     local[7].wait()
+    local[10].wait()
+    local[11].wait()
+    length = length_s[0]
+    weight = skip_v[...]
     arrive(GATE)
     row_ids = lax.broadcasted_iota(jnp.int32, (group, HD), 0)
     lane_ids = lax.broadcasted_iota(jnp.int32, (group, HD), 1)
@@ -399,23 +409,14 @@
             h_buf[: g + 1].reshape(width, HD),
             preferred_element_type=jnp.float32,
         )
-        a_buf[g] = (update / totals).astype(jnp.bfloat16)
+        attended = update / totals
+        a_buf[g] = attended.astype(jnp.bfloat16)
+        sq_mine[g : g + 1] = jnp.sum((attended * attended).T, axis=0, keepdims=True)
 
         @pl.when(me != g)
         def _():
             attended_copy(g, me).start()
 
-    a_in[me] = a_buf[me]
-    for step in range(1, ranks):
-        peer = lax.rem(me + step, ranks)
-        attended_copy(peer, peer).wait_recv()
-
-    squares = jnp.zeros((group, HD), jnp.float32)
-    for s in range(ranks):
-        piece = a_in[s].astype(jnp.float32)
-        squares = squares + piece * piece
-    row_squares = jnp.sum(squares.T, axis=0, keepdims=True)
-    sq_mine[...] = jnp.broadcast_to(row_squares, sq_mine.shape)
     for step in range(1, depth):
         other = lax.rem(plane + step, depth)
         copy = pltpu.make_async_remote_copy(
@@ -428,7 +429,8 @@
         )
         copy.start()
         sends.append(copy)
-    total_squares = sq_mine[:1]
+    a_in[me] = a_buf[me]
+    slot_squares = sq_mine[...]
     for step in range(1, depth):
         other = lax.rem(plane + step, depth)
         pltpu.make_async_remote_copy(
@@ -439,10 +441,39 @@
             device_id={"tp": other},
             device_id_type=MESH,
         ).wait_recv()
-        total_squares = total_squares + sq_in[other][:1]
-    inverse_norm = lax.rsqrt(total_squares * (1.0 / (depth * ranks * HD)) + 1e-06)
+        slot_squares = slot_squares + sq_in[other]
+    for g in range(ranks):
+        sq_sum[g] = jnp.broadcast_to(slot_squares[g : g + 1], sq_sum.shape[1:])
+    for step in range(1, ranks):
+        peer = lax.rem(me + step, ranks)
+        copy = pltpu.make_async_remote_copy(
+            src_ref=sq_sum.at[peer],
+            dst_ref=sq_got.at[me],
+            send_sem=total_send.at[step],
+            recv_sem=total_recv.at[me],
+            device_id={"ctx": peer},
+            device_id_type=MESH,
+        )
+        copy.start()
+        sends.append(copy)
+    total_squares = sq_sum[me]
+    for step in range(1, ranks):
+        peer = lax.rem(me + step, ranks)
+        pltpu.make_async_remote_copy(
+            src_ref=sq_sum.at[peer],
+            dst_ref=sq_got.at[peer],
+            send_sem=total_send.at[step],
+            recv_sem=total_recv.at[peer],
+            device_id={"ctx": peer},
+            device_id_type=MESH,
+        ).wait_recv()
+        total_squares = total_squares + sq_got[peer]
+    inverse_norm = lax.rsqrt(total_squares[:1] * (1.0 / (depth * ranks * HD)) + 1e-06)
     by_row = jnp.broadcast_to(inverse_norm, (group, HD)).T
     by_row = jnp.where(row_ids + me * group < length, by_row, 0.0)
+    for step in range(1, ranks):
+        peer = lax.rem(me + step, ranks)
+        attended_copy(peer, peer).wait_recv()
     for s in range(ranks):
         a_out[:, s * HD : (s + 1) * HD] = (a_in[s].astype(jnp.float32) * by_row).astype(
             jnp.bfloat16
@@ -473,14 +504,14 @@
     bf16, f32 = jnp.bfloat16, jnp.float32
     any_space = pl.BlockSpec(memory_space=pl.ANY)
     vmem = pl.BlockSpec(memory_space=pltpu.VMEM)
-    smem = pl.BlockSpec(memory_space=pltpu.SMEM)
+    hbm = pl.BlockSpec(memory_space=pltpu.HBM)
     return pl.pallas_call(
         functools.partial(head_kernel, ranks, depth),
         out_shape=(
             jax.ShapeDtypeStruct((group, channels), bf16),
             jax.ShapeDtypeStruct((group, channels), bf16),
         ),
-        in_specs=[any_space] * 4 + [vmem] + [any_space] * 2 + [smem] + [any_space] * 4,
+        in_specs=[hbm] * 12,
         out_specs=(any_space, vmem),
         scratch_shapes=[
             pltpu.VMEM((group, channels), bf16),
@@ -499,9 +530,13 @@
             pltpu.VMEM((ranks, group, HD), bf16),
             pltpu.VMEM((ranks, group, HD), bf16),
             pltpu.VMEM((ranks, group, HD), bf16),
-            pltpu.VMEM((8, group), f32),
-            pltpu.VMEM((depth, 8, group), f32),
-            pltpu.SemaphoreType.DMA((10,)),
+            pltpu.VMEM((1, HD), f32),
+            pltpu.SMEM((1,), jnp.int32),
+            pltpu.VMEM((ranks, group), f32),
+            pltpu.VMEM((depth, ranks, group), f32),
+            pltpu.VMEM((ranks, 8, group), f32),
+            pltpu.VMEM((ranks, 8, group), f32),
+            pltpu.SemaphoreType.DMA((12,)),
             pltpu.SemaphoreType.DMA((4, ranks)),
             pltpu.SemaphoreType.DMA((4, ranks)),
             pltpu.SemaphoreType.DMA((ranks,)),
@@ -510,9 +545,11 @@
             pltpu.SemaphoreType.DMA((ranks,)),
             pltpu.SemaphoreType.DMA((depth,)),
             pltpu.SemaphoreType.DMA((depth,)),
+            pltpu.SemaphoreType.DMA((ranks,)),
+            pltpu.SemaphoreType.DMA((ranks,)),
         ],
         compiler_params=pltpu.CompilerParams(
-            collective_id=0, has_side_effects=True, vmem_limit_bytes=40 * 1024 * 1024
+            collective_id=0, has_side_effects=True, vmem_limit_bytes=62 * 1024 * 1024
         ),
     )(
         hyena_key,

time: 45.5 us -> 36.9 us (0.81)
  local copies, waits for them, and re-layouts: 12.4 us -> 3.34 us
  Pallas kernels: 31.3 us -> 32 us
    unnamed x24 -> x2, local copies, waits for them, and re-layouts: 12.4 us -> 3.34 us
    pallas_call x1, Pallas kernels: 31.3 us -> 32 us  [head_shards(): pl.pallas_call(functools.partial(head_kernel, ranks, depth), out_shape=(j...]
where the time goes in v1:
time: 36.9 us; the launch traced here: 36.7 us
  Pallas kernels  32 us (87%)
  local copies, waits for them, and re-layouts  3.34 us (9%)
  between operations  1.29 us (3%)
    pallas_call x1, Pallas kernels, head_shards(): pl.pallas_call(functools.partial(head_kernel, ranks, depth), out_shape=(j...  32 us
    unnamed x2, local copies, waits for them, and re-layouts  3.34 us

profile of v1, /device:TPU:0, one launch (start us, length us, event | category | flops | bytes accessed | tf_op | source)
XLA Modules:
  0.0 36.7 jit_solution(11919591014426306932)
XLA Ops:
  1.3 32.0 %shard_map.131 = (bf16[128,1024]{1,0:T(8,128)(2,1)}, bf16[128,1024]{1,0:T(8,128)(2,1)}) custom-call(bf16[128,1024]{1,0:T(8,128)(2,1)} %hk.1, bf16[128,1024]{1,0:T(8,128)(2,1)} %hv.1, bf16[128,1024]{1,0:T(8,128)(2,1)} %gate.1, bf16[1024,1024]{1,0:T(8,128)(2,1)} %taps.1, f32[1,1024]{1,0:T(1,128)} %bitcast.1, bf16[128,1024]{1,0:T(8,128)(2,1)} %queries.1, ...), custom_call_target="tpu_custom_call" | custom-call | tf_op jit(solution)/shard_map/pallas_call | solution.py:508
  33.3 1.7 %copy.17 = bf16[128,1024]{1,0:T(8,128)(2,1)} copy(bf16[128,1024]{1,0:T(8,128)(2,1)} %get-tuple-element.4) | data formatting | bytes 524288
  35.0 1.7 %copy.18 = bf16[128,1024]{1,0:T(8,128)(2,1)} copy(bf16[128,1024]{1,0:T(8,128)(2,1)} %get-tuple-element.5) | data formatting | bytes 524288

commit v2 on v1

--- a/solution.py
+++ b/solution.py
@@ -180,6 +180,7 @@
     back_low,
     h_out,
     a_out,
+    norm_out,
     hk_v,
     hv_v,
     mix_v,
@@ -195,7 +196,6 @@
     sum_low,
     h_buf,
     a_buf,
-    a_in,
     skip_v,
     length_s,
     sq_mine,
@@ -377,21 +377,19 @@
     local[8].wait()
     local[9].wait()
     arrive(KEY)
-    arrive(QUERY)
     factor = math.log2(math.e) / math.sqrt(HD)
-    order = [g for low in range(per_block - 1, -1, -1) for g in range(ranks - per_block + low, -1, -per_block)]
 
     def attended_copy(g, source):
         return pltpu.make_async_remote_copy(
             src_ref=a_buf.at[g],
-            dst_ref=a_in.at[source],
+            dst_ref=a_out.at[:, columns(source)],
             send_sem=a_send.at[g],
             recv_sem=a_recv.at[source],
             device_id={"ctx": g},
             device_id_type=MESH,
         )
 
-    for g in order:
+    def attend_group(g):
         width = (g + 1) * group
         score = lax.dot_general(
             got[QUERY, g],
@@ -413,10 +411,33 @@
         a_buf[g] = attended.astype(jnp.bfloat16)
         sq_mine[g : g + 1] = jnp.sum((attended * attended).T, axis=0, keepdims=True)
 
-        @pl.when(me != g)
+    def attend(step, carry):
+        g = lax.rem(me + ranks - step, ranks)
+
+        @pl.when(step > 0)
+        def _():
+            pltpu.make_async_remote_copy(
+                src_ref=got.at[QUERY, g],
+                dst_ref=got.at[QUERY, g],
+                send_sem=in_send.at[QUERY, g],
+                recv_sem=in_recv.at[QUERY, g],
+                device_id={"ctx": g},
+                device_id_type=MESH,
+            ).wait_recv()
+
+        for index in range(ranks):
+
+            @pl.when(g == index)
+            def _():
+                attend_group(index)
+
+        @pl.when(step > 0)
         def _():
             attended_copy(g, me).start()
 
+        return carry
+
+    lax.fori_loop(0, ranks, attend, 0)
     for step in range(1, depth):
         other = lax.rem(plane + step, depth)
         copy = pltpu.make_async_remote_copy(
@@ -429,7 +450,8 @@
         )
         copy.start()
         sends.append(copy)
-    a_in[me] = a_buf[me]
+    a_local = pltpu.make_async_copy(a_buf.at[me], a_out.at[:, own], local_sem.at[1])
+    a_local.start()
     slot_squares = sq_mine[...]
     for step in range(1, depth):
         other = lax.rem(plane + step, depth)
@@ -470,15 +492,11 @@
         total_squares = total_squares + sq_got[peer]
     inverse_norm = lax.rsqrt(total_squares[:1] * (1.0 / (depth * ranks * HD)) + 1e-06)
     by_row = jnp.broadcast_to(inverse_norm, (group, HD)).T
-    by_row = jnp.where(row_ids + me * group < length, by_row, 0.0)
+    norm_out[...] = jnp.where(row_ids + me * group < length, by_row, 0.0)
     for step in range(1, ranks):
         peer = lax.rem(me + step, ranks)
         attended_copy(peer, peer).wait_recv()
-    for s in range(ranks):
-        a_out[:, s * HD : (s + 1) * HD] = (a_in[s].astype(jnp.float32) * by_row).astype(
-            jnp.bfloat16
-        )
-
+    a_local.wait()
     h_local.wait()
     for step in range(1, ranks):
         peer = lax.rem(me + step, ranks)
@@ -495,6 +513,13 @@
         copy.wait_send()
 
 
+def finish_kernel(h_rows, attended, norm, h_out, a_out):
+    h_out[...] = h_rows[...]
+    for first in range(0, attended.shape[1], HD):
+        lanes = slice(first, first + HD)
+        a_out[:, lanes] = (attended[:, lanes].astype(jnp.float32) * norm[...]).astype(jnp.bfloat16)
+
+
 def head_shards(ranks, depth, *arrays):
     hyena_gate, hyena_key, hyena_value, filter_taps, skip_weight, queries, attn_keys, valid = arrays
     group, channels = hyena_gate.shape
@@ -505,14 +530,15 @@
     any_space = pl.BlockSpec(memory_space=pl.ANY)
     vmem = pl.BlockSpec(memory_space=pltpu.VMEM)
     hbm = pl.BlockSpec(memory_space=pltpu.HBM)
-    return pl.pallas_call(
+    h_rows, attended, norm = pl.pallas_call(
         functools.partial(head_kernel, ranks, depth),
         out_shape=(
             jax.ShapeDtypeStruct((group, channels), bf16),
             jax.ShapeDtypeStruct((group, channels), bf16),
+            jax.ShapeDtypeStruct((group, HD), f32),
         ),
         in_specs=[hbm] * 12,
-        out_specs=(any_space, vmem),
+        out_specs=(any_space, any_space, vmem),
         scratch_shapes=[
             pltpu.VMEM((group, channels), bf16),
             pltpu.VMEM((group, channels), bf16),
@@ -527,7 +553,6 @@
             pltpu.VMEM((2 * block, blocks * HD), f32),
             pltpu.VMEM((2 * block, blocks * HD), bf16),
             pltpu.VMEM((2 * block, blocks * HD), bf16),
-            pltpu.VMEM((ranks, group, HD), bf16),
             pltpu.VMEM((ranks, group, HD), bf16),
             pltpu.VMEM((ranks, group, HD), bf16),
             pltpu.VMEM((1, HD), f32),
@@ -562,6 +587,15 @@
         valid,
         *(jnp.asarray(table) for table in half_shift_tables(block)),
     )
+    return pl.pallas_call(
+        finish_kernel,
+        out_shape=(
+            jax.ShapeDtypeStruct((group, channels), bf16),
+            jax.ShapeDtypeStruct((group, channels), bf16),
+        ),
+        in_specs=[vmem] * 3,
+        out_specs=(vmem, vmem),
+    )(h_rows, attended, norm)
 
 
 def solution(mesh):

time: 36.9 us -> 32.7 us (0.89)
  local copies, waits for them, and re-layouts: 3.34 us -> 0 us
  Pallas kernels: 32 us -> 31.3 us
    unnamed x2 -> x0, local copies, waits for them, and re-layouts: 3.34 us -> none
    pallas_call x1, Pallas kernels: 32 us -> 29.4 us  [head_shards(): pl.pallas_call(functools.partial(head_kernel, ranks, depth), out_shape=(j...]
    pallas_call x0 -> x1, Pallas kernels: none -> 1.84 us  [head_shards(): pl.pallas_call(finish_kernel, out_shape=(jax.ShapeDtypeStruct((group, cha...]
where the time goes in v2:
time: 32.7 us; the launch traced here: 32.6 us
  Pallas kernels  31.3 us (96%)
  between operations  1.29 us (4%)
    pallas_call x1, Pallas kernels, head_shards(): pl.pallas_call(functools.partial(head_kernel, ranks, depth), out_shape=(j...  29.4 us
    pallas_call x1, Pallas kernels, head_shards(): pl.pallas_call(finish_kernel, out_shape=(jax.ShapeDtypeStruct((group, cha...  1.84 us

profile of v2, /device:TPU:0, one launch (start us, length us, event | category | flops | bytes accessed | tf_op | source)
XLA Modules:
  0.0 32.6 jit_solution(10410076910496738927)
XLA Ops:
  1.3 29.4 %shard_map.131 = (bf16[128,1024]{1,0:T(8,128)(2,1)}, bf16[128,1024]{1,0:T(8,128)(2,1)}, f32[128,128]{1,0:T(8,128)}) custom-call(bf16[128,1024]{1,0:T(8,128)(2,1)} %hk.1, bf16[128,1024]{1,0:T(8,128)(2,1)} %hv.1, bf16[128,1024]{1,0:T(8,128)(2,1)} %gate.1, bf16[1024,1024]{1,0:T(8,128)(2,1)} %taps.1, f32[1,1024]{1,0:T(1,128)} %bitcast.1, ...), custom_call_target="tpu_custom_call" | custom-call | tf_op jit(solution)/shard_map/pallas_call | solution.py:533
  30.7 1.8 %shard_map.132 = (bf16[128,1024]{1,0:T(8,128)(2,1)}, bf16[128,1024]{1,0:T(8,128)(2,1)}) custom-call(bf16[128,1024]{1,0:T(8,128)(2,1)} %get-tuple-element.5.h_rows, bf16[128,1024]{1,0:T(8,128)(2,1)} %get-tuple-element.6.attended, f32[128,128]{1,0:T(8,128)} %get-tuple-element.7.norm), custom_call_target="tpu_custom_call" | custom-call | tf_op jit(solution)/shard_map/pallas_call | solution.py:590

commit v3 on v2

--- a/solution.py
+++ b/solution.py
@@ -183,7 +183,11 @@
     norm_out,
     hk_v,
     hv_v,
-    mix_v,
+    gate_v,
+    key_v,
+    query_v,
+    stage,
+    h_t,
     taps_v,
     ah_v,
     al_v,
@@ -237,9 +241,9 @@
                 (ahead_low, al_v),
                 (back_high, bh_v),
                 (back_low, bl_v),
-                (gate.at[:, own], got.at[GATE, me]),
-                (keys.at[:, own], got.at[KEY, me]),
-                (queries.at[:, own], got.at[QUERY, me]),
+                (gate, gate_v),
+                (keys, key_v),
+                (queries, query_v),
                 (skip.at[:, own], skip_v),
                 (valid, length_s),
             )
@@ -259,17 +263,23 @@
         )
     local[0].wait()
     local[1].wait()
-    mix_v[...] = (hk_v[...].astype(jnp.float32) * hv_v[...].astype(jnp.float32)).astype(
-        jnp.bfloat16
-    )
+    for p in range(ranks):
+        lanes = slice(p * HD, (p + 1) * HD)
+        stage[MIX, p] = (
+            hk_v[:, lanes].astype(jnp.float32) * hv_v[:, lanes].astype(jnp.float32)
+        ).astype(jnp.bfloat16)
     pl.semaphore_wait(barrier, ranks - 1 + depth - 1)
 
     sends = []
-    for which, src in ((MIX, mix_v), (GATE, gate), (KEY, keys), (QUERY, queries)):
+    for which, src in ((MIX, None), (GATE, gate_v), (KEY, key_v), (QUERY, query_v)):
+        if src is not None:
+            local[6 + which].wait()
+            for p in range(ranks):
+                stage[which, p] = src[:, p * HD : (p + 1) * HD]
         for step in range(1, ranks):
             peer = lax.rem(me + step, ranks)
             copy = pltpu.make_async_remote_copy(
-                src_ref=src.at[:, columns(peer)],
+                src_ref=stage.at[which, peer],
                 dst_ref=got.at[which, me],
                 send_sem=in_send.at[which, step],
                 recv_sem=in_recv.at[which, me],
@@ -291,7 +301,8 @@
                 device_id_type=MESH,
             ).wait_recv()
 
-    got[MIX, me] = mix_v[:, own]
+    for which in range(4):
+        got[which, me] = stage[which, me]
     taps_v[:block] = jnp.zeros((block, HD), jnp.bfloat16)
     for copy in local[2:7]:
         copy.wait()
@@ -341,7 +352,6 @@
         + jnp.dot(bh_v[...], sum_low[...], preferred_element_type=jnp.float32)
     )
 
-    local[7].wait()
     local[10].wait()
     local[11].wait()
     length = length_s[0]
@@ -374,8 +384,10 @@
         copy.start()
         sends.append(copy)
 
-    local[8].wait()
-    local[9].wait()
+    for g in range(ranks):
+        h_t[:, g * group : (g + 1) * group] = (
+            h_buf[g].astype(jnp.float32).T.astype(jnp.bfloat16)
+        )
     arrive(KEY)
     factor = math.log2(math.e) / math.sqrt(HD)
 
@@ -392,24 +404,22 @@
     def attend_group(g):
         width = (g + 1) * group
         score = lax.dot_general(
+            got[KEY, : g + 1].reshape(width, HD),
             got[QUERY, g],
-            got[KEY, : g + 1].reshape(width, HD),
             (((1,), (1,)), ((), ())),
             preferred_element_type=jnp.float32,
         )
-        last = jnp.where(lane_ids <= row_ids, score[:, g * group :], -1e30)
-        score = last if g == 0 else jnp.concatenate([score[:, : g * group], last], axis=1)
-        row_max = jnp.max(score, axis=1, keepdims=True)
+        last = jnp.where(row_ids <= lane_ids, score[g * group :], -1e30)
+        score = last if g == 0 else jnp.concatenate([score[: g * group], last], axis=0)
+        row_max = jnp.max(score, axis=0, keepdims=True)
         raw = jnp.exp2((score - row_max) * factor)
-        totals = jnp.sum(raw, axis=1, keepdims=True)
+        totals = jnp.sum(raw, axis=0, keepdims=True)
         update = jnp.dot(
-            raw.astype(jnp.bfloat16),
-            h_buf[: g + 1].reshape(width, HD),
-            preferred_element_type=jnp.float32,
+            h_t[:, :width], raw.astype(jnp.bfloat16), preferred_element_type=jnp.float32
         )
         attended = update / totals
-        a_buf[g] = attended.astype(jnp.bfloat16)
-        sq_mine[g : g + 1] = jnp.sum((attended * attended).T, axis=0, keepdims=True)
+        a_buf[g] = attended.T.astype(jnp.bfloat16)
+        sq_mine[g : g + 1] = jnp.sum(attended * attended, axis=0, keepdims=True)
 
     def attend(step, carry):
         g = lax.rem(me + ranks - step, ranks)
@@ -543,6 +553,10 @@
             pltpu.VMEM((group, channels), bf16),
             pltpu.VMEM((group, channels), bf16),
             pltpu.VMEM((group, channels), bf16),
+            pltpu.VMEM((group, channels), bf16),
+            pltpu.VMEM((group, channels), bf16),
+            pltpu.VMEM((4, ranks, group, HD), bf16),
+            pltpu.VMEM((HD, seq), bf16),
             pltpu.VMEM((block + seq, HD), bf16),
             pltpu.VMEM((2 * block, 2 * block), bf16),
             pltpu.VMEM((2 * block, 2 * block), bf16),

time: 32.7 us -> 32.8 us (level)
  no operation moved by 1% of the time
where the time goes in v3:
time: 32.8 us; the launch traced here: 32.6 us
  Pallas kernels  31.4 us (96%)
  between operations  1.29 us (4%)
    pallas_call x1, Pallas kernels, head_shards(): pl.pallas_call(functools.partial(head_kernel, ranks, depth), out_shape=(j...  29.5 us
    pallas_call x1, Pallas kernels, head_shards(): pl.pallas_call(finish_kernel, out_shape=(jax.ShapeDtypeStruct((group, cha...  1.84 us

profile of v3, /device:TPU:0, one launch (start us, length us, event | category | flops | bytes accessed | tf_op | source)
XLA Modules:
  0.0 32.6 jit_solution(7752004549673802206)
XLA Ops:
  1.3 29.5 %shard_map.131 = (bf16[128,1024]{1,0:T(8,128)(2,1)}, bf16[128,1024]{1,0:T(8,128)(2,1)}, f32[128,128]{1,0:T(8,128)}) custom-call(bf16[128,1024]{1,0:T(8,128)(2,1)} %hk.1, bf16[128,1024]{1,0:T(8,128)(2,1)} %hv.1, bf16[128,1024]{1,0:T(8,128)(2,1)} %gate.1, bf16[1024,1024]{1,0:T(8,128)(2,1)} %taps.1, f32[1,1024]{1,0:T(1,128)} %bitcast.1, ...), custom_call_target="tpu_custom_call" | custom-call | tf_op jit(solution)/shard_map/pallas_call | solution.py:543
  30.8 1.8 %shard_map.132 = (bf16[128,1024]{1,0:T(8,128)(2,1)}, bf16[128,1024]{1,0:T(8,128)(2,1)}) custom-call(bf16[128,1024]{1,0:T(8,128)(2,1)} %get-tuple-element.5.h_rows, bf16[128,1024]{1,0:T(8,128)(2,1)} %get-tuple-element.6.attended, f32[128,128]{1,0:T(8,128)} %get-tuple-element.7.norm), custom_call_target="tpu_custom_call" | custom-call | tf_op jit(solution)/shard_map/pallas_call | solution.py:604

commit v4 on v3

--- a/solution.py
+++ b/solution.py
@@ -271,7 +271,8 @@
     pl.semaphore_wait(barrier, ranks - 1 + depth - 1)
 
     sends = []
-    for which, src in ((MIX, None), (GATE, gate_v), (KEY, key_v), (QUERY, query_v)):
+
+    def send(which, src):
         if src is not None:
             local[6 + which].wait()
             for p in range(ranks):
@@ -288,6 +289,9 @@
             )
             copy.start()
             sends.append(copy)
+        got[which, me] = stage[which, me]
+
+    send(MIX, None)
 
     def arrive(which):
         for step in range(1, ranks):
@@ -301,8 +305,6 @@
                 device_id_type=MESH,
             ).wait_recv()
 
-    for which in range(4):
-        got[which, me] = stage[which, me]
     taps_v[:block] = jnp.zeros((block, HD), jnp.bfloat16)
     for copy in local[2:7]:
         copy.wait()
@@ -313,7 +315,10 @@
         al_v[...], windows, preferred_element_type=jnp.float32
     )
 
+    send(GATE, gate_v)
     arrive(MIX)
+    send(KEY, key_v)
+    send(QUERY, query_v)
     mixed = got[MIX].reshape(seq, HD)
     inputs = jnp.concatenate([mixed[i * block : (i + 1) * block] for i in range(blocks)], axis=1)
     in_s[...] = jnp.dot(
@@ -345,7 +350,7 @@
                 sum_low[rows, lanes[i]] = (total - high.astype(jnp.float32)).astype(jnp.bfloat16)
         return carry
 
-    lax.fori_loop(0, block // rows_at_once, multiply, 0)
+    lax.fori_loop(0, block // rows_at_once, multiply, 0, unroll=4)
     convolved = (
         jnp.dot(bh_v[...], sum_high[...], preferred_element_type=jnp.float32)
         + jnp.dot(bl_v[...], sum_high[...], preferred_element_type=jnp.float32)

time: 32.8 us -> 32.6 us (level)
  no operation moved by 1% of the time
where the time goes in v4:
time: 32.6 us; the launch traced here: 32.5 us
  Pallas kernels  31.2 us (96%)
  between operations  1.29 us (4%)
    pallas_call x1, Pallas kernels, head_shards(): pl.pallas_call(functools.partial(head_kernel, ranks, depth), out_shape=(j...  29.3 us
    pallas_call x1, Pallas kernels, head_shards(): pl.pallas_call(finish_kernel, out_shape=(jax.ShapeDtypeStruct((group, cha...  1.84 us

profile of v4, /device:TPU:0, one launch (start us, length us, event | category | flops | bytes accessed | tf_op | source)
XLA Modules:
  0.0 32.5 jit_solution(10978113716468522027)
XLA Ops:
  1.3 29.3 %shard_map.131 = (bf16[128,1024]{1,0:T(8,128)(2,1)}, bf16[128,1024]{1,0:T(8,128)(2,1)}, f32[128,128]{1,0:T(8,128)}) custom-call(bf16[128,1024]{1,0:T(8,128)(2,1)} %hk.1, bf16[128,1024]{1,0:T(8,128)(2,1)} %hv.1, bf16[128,1024]{1,0:T(8,128)(2,1)} %gate.1, bf16[1024,1024]{1,0:T(8,128)(2,1)} %taps.1, f32[1,1024]{1,0:T(1,128)} %bitcast.1, ...), custom_call_target="tpu_custom_call" | custom-call | tf_op jit(solution)/shard_map/pallas_call | solution.py:548
  30.6 1.8 %shard_map.132 = (bf16[128,1024]{1,0:T(8,128)(2,1)}, bf16[128,1024]{1,0:T(8,128)(2,1)}) custom-call(bf16[128,1024]{1,0:T(8,128)(2,1)} %get-tuple-element.5.h_rows, bf16[128,1024]{1,0:T(8,128)(2,1)} %get-tuple-element.6.attended, f32[128,128]{1,0:T(8,128)} %get-tuple-element.7.norm), custom_call_target="tpu_custom_call" | custom-call | tf_op jit(solution)/shard_map/pallas_call | solution.py:609

commit v5 on v4

--- a/solution.py
+++ b/solution.py
@@ -229,6 +229,19 @@
     def columns(index):
         return pl.ds(pl.multiple_of(index * HD, HD), HD)
 
+    core, across, along = lax.rem(me, 2), lax.rem(lax.div(me, 2), 2), lax.div(me, 4)
+
+    def partner(step):
+        if ranks != 8:
+            return lax.rem(me + step, ranks)
+        step = jnp.asarray(step, jnp.int32)
+        kind = lax.rem(step, 4)
+        low, high = lax.rem(kind, 2), lax.div(kind, 2)
+        dx = low * (1 - core) + high * core
+        dy = high * (1 - core) + low * core
+        chip = lax.rem(along + dy, 2) * 2 + lax.rem(across + dx, 2)
+        return chip * 2 + lax.rem(core + lax.div(step, 4), 2)
+
     own = columns(me)
     local = [
         pltpu.make_async_copy(src, dst, local_sem.at[i])
@@ -255,7 +268,7 @@
     barrier = pltpu.get_barrier_semaphore()
     for step in range(1, ranks):
         pl.semaphore_signal(
-            barrier, inc=1, device_id={"ctx": lax.rem(me + step, ranks)}, device_id_type=MESH
+            barrier, inc=1, device_id={"ctx": partner(step)}, device_id_type=MESH
         )
     for step in range(1, depth):
         pl.semaphore_signal(
@@ -278,7 +291,7 @@
             for p in range(ranks):
                 stage[which, p] = src[:, p * HD : (p + 1) * HD]
         for step in range(1, ranks):
-            peer = lax.rem(me + step, ranks)
+            peer = partner(step)
             copy = pltpu.make_async_remote_copy(
                 src_ref=stage.at[which, peer],
                 dst_ref=got.at[which, me],
@@ -295,7 +308,7 @@
 
     def arrive(which):
         for step in range(1, ranks):
-            peer = lax.rem(me + step, ranks)
+            peer = partner(step)
             pltpu.make_async_remote_copy(
                 src_ref=got.at[which, peer],
                 dst_ref=got.at[which, peer],
@@ -377,7 +390,7 @@
     h_local = pltpu.make_async_copy(h_buf.at[me], h_out.at[:, own], local_sem.at[0])
     h_local.start()
     for step in range(1, ranks):
-        peer = lax.rem(me + step, ranks)
+        peer = partner(step)
         copy = pltpu.make_async_remote_copy(
             src_ref=h_buf.at[peer],
             dst_ref=h_out.at[:, own],
@@ -427,7 +440,7 @@
         sq_mine[g : g + 1] = jnp.sum(attended * attended, axis=0, keepdims=True)
 
     def attend(step, carry):
-        g = lax.rem(me + ranks - step, ranks)
+        g = partner(step)
 
         @pl.when(step > 0)
         def _():
@@ -482,7 +495,7 @@
     for g in range(ranks):
         sq_sum[g] = jnp.broadcast_to(slot_squares[g : g + 1], sq_sum.shape[1:])
     for step in range(1, ranks):
-        peer = lax.rem(me + step, ranks)
+        peer = partner(step)
         copy = pltpu.make_async_remote_copy(
             src_ref=sq_sum.at[peer],
             dst_ref=sq_got.at[me],
@@ -495,7 +508,7 @@
         sends.append(copy)
     total_squares = sq_sum[me]
     for step in range(1, ranks):
-        peer = lax.rem(me + step, ranks)
+        peer = partner(step)
         pltpu.make_async_remote_copy(
             src_ref=sq_sum.at[peer],
             dst_ref=sq_got.at[peer],
@@ -509,12 +522,12 @@
     by_row = jnp.broadcast_to(inverse_norm, (group, HD)).T
     norm_out[...] = jnp.where(row_ids + me * group < length, by_row, 0.0)
     for step in range(1, ranks):
-        peer = lax.rem(me + step, ranks)
+        peer = partner(step)
         attended_copy(peer, peer).wait_recv()
     a_local.wait()
     h_local.wait()
     for step in range(1, ranks):
-        peer = lax.rem(me + step, ranks)
+        peer = partner(step)
         pltpu.make_async_remote_copy(
             src_ref=h_buf.at[peer],
             dst_ref=h_out.at[:, columns(peer)],

time: 32.6 us -> 33.2 us (1.018)
  Pallas kernels: 31.2 us -> 31.8 us
    pallas_call x1, Pallas kernels: 29.3 us -> 29.9 us  [head_shards(): pl.pallas_call(functools.partial(head_kernel, ranks, depth), out_shape=(j...]
where the time goes in v5:
time: 33.2 us; the launch traced here: 33.1 us
  Pallas kernels  31.8 us (96%)
  between operations  1.29 us (4%)
    pallas_call x1, Pallas kernels, head_shards(): pl.pallas_call(functools.partial(head_kernel, ranks, depth), out_shape=(j...  29.9 us
    pallas_call x1, Pallas kernels, head_shards(): pl.pallas_call(finish_kernel, out_shape=(jax.ShapeDtypeStruct((group, cha...  1.84 us

profile of v5, /device:TPU:0, one launch (start us, length us, event | category | flops | bytes accessed | tf_op | source)
XLA Modules:
  0.0 33.1 jit_solution(18107697436130030163)
XLA Ops:
  1.3 29.9 %shard_map.131 = (bf16[128,1024]{1,0:T(8,128)(2,1)}, bf16[128,1024]{1,0:T(8,128)(2,1)}, f32[128,128]{1,0:T(8,128)}) custom-call(bf16[128,1024]{1,0:T(8,128)(2,1)} %hk.1, bf16[128,1024]{1,0:T(8,128)(2,1)} %hv.1, bf16[128,1024]{1,0:T(8,128)(2,1)} %gate.1, bf16[1024,1024]{1,0:T(8,128)(2,1)} %taps.1, f32[1,1024]{1,0:T(1,128)} %bitcast.1, ...), custom_call_target="tpu_custom_call" | custom-call | tf_op jit(solution)/shard_map/pallas_call | solution.py:561
  31.2 1.8 %shard_map.132 = (bf16[128,1024]{1,0:T(8,128)(2,1)}, bf16[128,1024]{1,0:T(8,128)(2,1)}) custom-call(bf16[128,1024]{1,0:T(8,128)(2,1)} %get-tuple-element.5.h_rows, bf16[128,1024]{1,0:T(8,128)(2,1)} %get-tuple-element.6.attended, f32[128,128]{1,0:T(8,128)} %get-tuple-element.7.norm), custom_call_target="tpu_custom_call" | custom-call | tf_op jit(solution)/shard_map/pallas_call | solution.py:622

commit v6 on v3

--- a/solution.py
+++ b/solution.py
@@ -145,7 +145,7 @@
 
 
 MESH = pl.DeviceIdType.MESH
-MIX, GATE, KEY, QUERY = range(4)
+EARLY, LATE = range(2)
 
 
 def half_shift_tables(block):
@@ -265,44 +265,56 @@
     local[1].wait()
     for p in range(ranks):
         lanes = slice(p * HD, (p + 1) * HD)
-        stage[MIX, p] = (
+        stage[EARLY, p, 0] = (
             hk_v[:, lanes].astype(jnp.float32) * hv_v[:, lanes].astype(jnp.float32)
         ).astype(jnp.bfloat16)
+    local[7].wait()
+    for p in range(ranks):
+        stage[EARLY, p, 1] = gate_v[:, p * HD : (p + 1) * HD]
     pl.semaphore_wait(barrier, ranks - 1 + depth - 1)
 
     sends = []
-    for which, src in ((MIX, None), (GATE, gate_v), (KEY, key_v), (QUERY, query_v)):
-        if src is not None:
-            local[6 + which].wait()
-            for p in range(ranks):
-                stage[which, p] = src[:, p * HD : (p + 1) * HD]
-        for step in range(1, ranks):
-            peer = lax.rem(me + step, ranks)
-            copy = pltpu.make_async_remote_copy(
-                src_ref=stage.at[which, peer],
-                dst_ref=got.at[which, me],
-                send_sem=in_send.at[which, step],
-                recv_sem=in_recv.at[which, me],
-                device_id={"ctx": peer},
-                device_id_type=MESH,
-            )
-            copy.start()
-            sends.append(copy)
-
-    def arrive(which):
+
+    def lay_out(bundle, which, src, ready):
+        ready.wait()
+        for p in range(ranks):
+            stage[bundle, p, which] = src[:, p * HD : (p + 1) * HD]
+
+    def send(bundle):
         for step in range(1, ranks):
             peer = lax.rem(me + step, ranks)
             pltpu.make_async_remote_copy(
-                src_ref=got.at[which, peer],
-                dst_ref=got.at[which, peer],
-                send_sem=in_send.at[which, step],
-                recv_sem=in_recv.at[which, peer],
+                src_ref=stage.at[bundle, peer],
+                dst_ref=got.at[bundle, me],
+                send_sem=in_send.at[bundle],
+                recv_sem=in_recv.at[bundle],
                 device_id={"ctx": peer},
                 device_id_type=MESH,
-            ).wait_recv()
-
-    for which in range(4):
-        got[which, me] = stage[which, me]
+            ).start()
+
+    def all_of(src, dst, send_sem, recv_sem):
+        return pltpu.make_async_remote_copy(
+            src_ref=src,
+            dst_ref=dst,
+            send_sem=send_sem,
+            recv_sem=recv_sem,
+            device_id={"ctx": lax.rem(me + 1, ranks)},
+            device_id_type=MESH,
+        )
+
+    others = pl.ds(0, ranks - 1)
+
+    def bundle_copies(bundle):
+        return all_of(
+            stage.at[bundle, others], got.at[bundle, others], in_send.at[bundle], in_recv.at[bundle]
+        )
+
+    send(EARLY)
+    lay_out(LATE, 0, key_v, local[8])
+    lay_out(LATE, 1, query_v, local[9])
+    send(LATE)
+    for bundle in (EARLY, LATE):
+        got[bundle, me] = stage[bundle, me]
     taps_v[:block] = jnp.zeros((block, HD), jnp.bfloat16)
     for copy in local[2:7]:
         copy.wait()
@@ -313,8 +325,8 @@
         al_v[...], windows, preferred_element_type=jnp.float32
     )
 
-    arrive(MIX)
-    mixed = got[MIX].reshape(seq, HD)
+    bundle_copies(EARLY).wait_recv()
+    mixed = got[EARLY, :, 0].reshape(seq, HD)
     inputs = jnp.concatenate([mixed[i * block : (i + 1) * block] for i in range(blocks)], axis=1)
     in_s[...] = jnp.dot(
         ah_v[:, block:], inputs, preferred_element_type=jnp.float32
@@ -345,7 +357,7 @@
                 sum_low[rows, lanes[i]] = (total - high.astype(jnp.float32)).astype(jnp.bfloat16)
         return carry
 
-    lax.fori_loop(0, block // rows_at_once, multiply, 0)
+    lax.fori_loop(0, block // rows_at_once, multiply, 0, unroll=4)
     convolved = (
         jnp.dot(bh_v[...], sum_high[...], preferred_element_type=jnp.float32)
         + jnp.dot(bl_v[...], sum_high[...], preferred_element_type=jnp.float32)
@@ -356,7 +368,6 @@
     local[11].wait()
     length = length_s[0]
     weight = skip_v[...]
-    arrive(GATE)
     row_ids = lax.broadcasted_iota(jnp.int32, (group, HD), 0)
     lane_ids = lax.broadcasted_iota(jnp.int32, (group, HD), 1)
     for g in range(ranks):
@@ -364,8 +375,8 @@
             g % per_block * group : (g % per_block + 1) * group,
             g // per_block * HD : (g // per_block + 1) * HD,
         ]
-        gated = got[GATE, g].astype(jnp.float32) * (
-            part + weight * got[MIX, g].astype(jnp.float32)
+        gated = got[EARLY, g, 1].astype(jnp.float32) * (
+            part + weight * got[EARLY, g, 0].astype(jnp.float32)
         )
         h_buf[g] = jnp.where(row_ids + g * group < length, gated, 0.0).astype(jnp.bfloat16)
 
@@ -373,30 +384,28 @@
     h_local.start()
     for step in range(1, ranks):
         peer = lax.rem(me + step, ranks)
-        copy = pltpu.make_async_remote_copy(
+        pltpu.make_async_remote_copy(
             src_ref=h_buf.at[peer],
             dst_ref=h_out.at[:, own],
-            send_sem=h_send.at[step],
-            recv_sem=h_recv.at[me],
+            send_sem=h_send,
+            recv_sem=h_recv,
             device_id={"ctx": peer},
             device_id_type=MESH,
-        )
-        copy.start()
-        sends.append(copy)
+        ).start()
 
     for g in range(ranks):
         h_t[:, g * group : (g + 1) * group] = (
             h_buf[g].astype(jnp.float32).T.astype(jnp.bfloat16)
         )
-    arrive(KEY)
+    bundle_copies(LATE).wait_recv()
     factor = math.log2(math.e) / math.sqrt(HD)
 
     def attended_copy(g, source):
         return pltpu.make_async_remote_copy(
             src_ref=a_buf.at[g],
             dst_ref=a_out.at[:, columns(source)],
-            send_sem=a_send.at[g],
-            recv_sem=a_recv.at[source],
+            send_sem=a_send,
+            recv_sem=a_recv,
             device_id={"ctx": g},
             device_id_type=MESH,
         )
@@ -404,8 +413,8 @@
     def attend_group(g):
         width = (g + 1) * group
         score = lax.dot_general(
-            got[KEY, : g + 1].reshape(width, HD),
-            got[QUERY, g],
+            got[LATE, : g + 1, 0].reshape(width, HD),
+            got[LATE, g, 1],
             (((1,), (1,)), ((), ())),
             preferred_element_type=jnp.float32,
         )
@@ -423,17 +432,6 @@
 
     def attend(step, carry):
         g = lax.rem(me + ranks - step, ranks)
-
-        @pl.when(step > 0)
-        def _():
-            pltpu.make_async_remote_copy(
-                src_ref=got.at[QUERY, g],
-                dst_ref=got.at[QUERY, g],
-                send_sem=in_send.at[QUERY, g],
-                recv_sem=in_recv.at[QUERY, g],
-                device_id={"ctx": g},
-                device_id_type=MESH,
-            ).wait_recv()
 
         for index in range(ranks):
 
@@ -478,47 +476,31 @@
         sq_sum[g] = jnp.broadcast_to(slot_squares[g : g + 1], sq_sum.shape[1:])
     for step in range(1, ranks):
         peer = lax.rem(me + step, ranks)
-        copy = pltpu.make_async_remote_copy(
+        pltpu.make_async_remote_copy(
             src_ref=sq_sum.at[peer],
             dst_ref=sq_got.at[me],
-            send_sem=total_send.at[step],
-            recv_sem=total_recv.at[me],
+            send_sem=total_send,
+            recv_sem=total_recv,
             device_id={"ctx": peer},
             device_id_type=MESH,
-        )
-        copy.start()
-        sends.append(copy)
+        ).start()
+    totals_copy = all_of(sq_sum.at[others], sq_got.at[others], total_send, total_recv)
+    totals_copy.wait_recv()
     total_squares = sq_sum[me]
     for step in range(1, ranks):
-        peer = lax.rem(me + step, ranks)
-        pltpu.make_async_remote_copy(
-            src_ref=sq_sum.at[peer],
-            dst_ref=sq_got.at[peer],
-            send_sem=total_send.at[step],
-            recv_sem=total_recv.at[peer],
-            device_id={"ctx": peer},
-            device_id_type=MESH,
-        ).wait_recv()
-        total_squares = total_squares + sq_got[peer]
+        total_squares = total_squares + sq_got[lax.rem(me + step, ranks)]
     inverse_norm = lax.rsqrt(total_squares[:1] * (1.0 / (depth * ranks * HD)) + 1e-06)
     by_row = jnp.broadcast_to(inverse_norm, (group, HD)).T
     norm_out[...] = jnp.where(row_ids + me * group < length, by_row, 0.0)
-    for step in range(1, ranks):
-        peer = lax.rem(me + step, ranks)
-        attended_copy(peer, peer).wait_recv()
+    most = pl.ds(0, (ranks - 1) * HD)
+    a_copies = all_of(a_buf.at[others], a_out.at[:, most], a_send, a_recv)
+    a_copies.wait_recv()
     a_local.wait()
     h_local.wait()
-    for step in range(1, ranks):
-        peer = lax.rem(me + step, ranks)
-        pltpu.make_async_remote_copy(
-            src_ref=h_buf.at[peer],
-            dst_ref=h_out.at[:, columns(peer)],
-            send_sem=h_send.at[step],
-            recv_sem=h_recv.at[peer],
-            device_id={"ctx": peer},
-            device_id_type=MESH,
-        ).wait_recv()
-        attended_copy(peer, me).wait_send()
+    h_copies = all_of(h_buf.at[others], h_out.at[:, most], h_send, h_recv)
+    h_copies.wait_recv()
+    for copies in (bundle_copies(EARLY), bundle_copies(LATE), h_copies, a_copies, totals_copy):
+        copies.wait_send()
     for copy in sends:
         copy.wait_send()
 
@@ -555,14 +537,14 @@
             pltpu.VMEM((group, channels), bf16),
             pltpu.VMEM((group, channels), bf16),
             pltpu.VMEM((group, channels), bf16),
-            pltpu.VMEM((4, ranks, group, HD), bf16),
+            pltpu.VMEM((2, ranks, 2, group, HD), bf16),
             pltpu.VMEM((HD, seq), bf16),
             pltpu.VMEM((block + seq, HD), bf16),
             pltpu.VMEM((2 * block, 2 * block), bf16),
             pltpu.VMEM((2 * block, 2 * block), bf16),
             pltpu.VMEM((block, 2 * block), bf16),
             pltpu.VMEM((block, 2 * block), bf16),
-            pltpu.VMEM((4, ranks, group, HD), bf16),
+            pltpu.VMEM((2, ranks, 2, group, HD), bf16),
             pltpu.VMEM((2 * block, blocks * HD), f32),
             pltpu.VMEM((2 * block, blocks * HD), f32),
             pltpu.VMEM((2 * block, blocks * HD), bf16),
@@ -576,16 +558,16 @@
             pltpu.VMEM((ranks, 8, group), f32),
             pltpu.VMEM((ranks, 8, group), f32),
             pltpu.SemaphoreType.DMA((12,)),
-            pltpu.SemaphoreType.DMA((4, ranks)),
-            pltpu.SemaphoreType.DMA((4, ranks)),
-            pltpu.SemaphoreType.DMA((ranks,)),
-            pltpu.SemaphoreType.DMA((ranks,)),
-            pltpu.SemaphoreType.DMA((ranks,)),
-            pltpu.SemaphoreType.DMA((ranks,)),
+            pltpu.SemaphoreType.DMA((2,)),
+            pltpu.SemaphoreType.DMA((2,)),
+            pltpu.SemaphoreType.DMA,
+            pltpu.SemaphoreType.DMA,
+            pltpu.SemaphoreType.DMA,
+            pltpu.SemaphoreType.DMA,
             pltpu.SemaphoreType.DMA((depth,)),
             pltpu.SemaphoreType.DMA((depth,)),
-            pltpu.SemaphoreType.DMA((ranks,)),
-            pltpu.SemaphoreType.DMA((ranks,)),
+            pltpu.SemaphoreType.DMA,
+            pltpu.SemaphoreType.DMA,
         ],
         compiler_params=pltpu.CompilerParams(
             collective_id=0, has_side_effects=True, vmem_limit_bytes=62 * 1024 * 1024

time: 32.8 us -> 34 us (1.037)
  Pallas kernels: 31.4 us -> 32.6 us
    pallas_call x1, Pallas kernels: 29.5 us -> 30.7 us  [head_shards(): pl.pallas_call(functools.partial(head_kernel, ranks, depth), out_shape=(j...]
where the time goes in v6:
time: 34 us; the launch traced here: 33.9 us
  Pallas kernels  32.6 us (96%)
  between operations  1.29 us (4%)
    pallas_call x1, Pallas kernels, head_shards(): pl.pallas_call(functools.partial(head_kernel, ranks, depth), out_shape=(j...  30.7 us
    pallas_call x1, Pallas kernels, head_shards(): pl.pallas_call(finish_kernel, out_shape=(jax.ShapeDtypeStruct((group, cha...  1.84 us

profile of v6, /device:TPU:0, one launch (start us, length us, event | category | flops | bytes accessed | tf_op | source)
XLA Modules:
  0.0 33.9 jit_solution(2007842364385756626)
XLA Ops:
  1.3 30.7 %shard_map.131 = (bf16[128,1024]{1,0:T(8,128)(2,1)}, bf16[128,1024]{1,0:T(8,128)(2,1)}, f32[128,128]{1,0:T(8,128)}) custom-call(bf16[128,1024]{1,0:T(8,128)(2,1)} %hk.1, bf16[128,1024]{1,0:T(8,128)(2,1)} %hv.1, bf16[128,1024]{1,0:T(8,128)(2,1)} %gate.1, bf16[1024,1024]{1,0:T(8,128)(2,1)} %taps.1, f32[1,1024]{1,0:T(1,128)} %bitcast.1, ...), custom_call_target="tpu_custom_call" | custom-call | tf_op jit(solution)/shard_map/pallas_call | solution.py:525
  32.0 1.8 %shard_map.132 = (bf16[128,1024]{1,0:T(8,128)(2,1)}, bf16[128,1024]{1,0:T(8,128)(2,1)}) custom-call(bf16[128,1024]{1,0:T(8,128)(2,1)} %get-tuple-element.5.h_rows, bf16[128,1024]{1,0:T(8,128)(2,1)} %get-tuple-element.6.attended, f32[128,128]{1,0:T(8,128)} %get-tuple-element.7.norm), custom_call_target="tpu_custom_call" | custom-call | tf_op jit(solution)/shard_map/pallas_call | solution.py:586

commit v7 on v4

--- a/solution.py
+++ b/solution.py
@@ -196,8 +196,7 @@
     got,
     lag_s,
     in_s,
-    sum_high,
-    sum_low,
+    sums,
     h_buf,
     a_buf,
     skip_v,
@@ -345,16 +344,12 @@
                 real = more_real if real is None else real + more_real
                 imag = more_imag if imag is None else imag + more_imag
             for rows, total in ((real_rows, real), (imag_rows, imag)):
-                high = total.astype(jnp.bfloat16)
-                sum_high[rows, lanes[i]] = high
-                sum_low[rows, lanes[i]] = (total - high.astype(jnp.float32)).astype(jnp.bfloat16)
+                sums[rows, lanes[i]] = total.astype(jnp.bfloat16)
         return carry
 
     lax.fori_loop(0, block // rows_at_once, multiply, 0, unroll=4)
-    convolved = (
-        jnp.dot(bh_v[...], sum_high[...], preferred_element_type=jnp.float32)
-        + jnp.dot(bl_v[...], sum_high[...], preferred_element_type=jnp.float32)
-        + jnp.dot(bh_v[...], sum_low[...], preferred_element_type=jnp.float32)
+    convolved = jnp.dot(bh_v[...], sums[...], preferred_element_type=jnp.float32) + jnp.dot(
+        bl_v[...], sums[...], preferred_element_type=jnp.float32
     )
 
     local[10].wait()
@@ -571,7 +566,6 @@
             pltpu.VMEM((2 * block, blocks * HD), f32),
             pltpu.VMEM((2 * block, blocks * HD), f32),
             pltpu.VMEM((2 * block, blocks * HD), bf16),
-            pltpu.VMEM((2 * block, blocks * HD), bf16),
             pltpu.VMEM((ranks, group, HD), bf16),
             pltpu.VMEM((ranks, group, HD), bf16),
             pltpu.VMEM((1, HD), f32),

time: 32.6 us -> 32.6 us (level)
  no operation moved by 1% of the time
where the time goes in v7:
time: 32.6 us; the launch traced here: 32.5 us
  Pallas kernels  31.2 us (96%)
  between operations  1.29 us (4%)
    pallas_call x1, Pallas kernels, head_shards(): pl.pallas_call(functools.partial(head_kernel, ranks, depth), out_shape=(j...  29.3 us
    pallas_call x1, Pallas kernels, head_shards(): pl.pallas_call(finish_kernel, out_shape=(jax.ShapeDtypeStruct((group, cha...  1.84 us

profile of v7, /device:TPU:0, one launch (start us, length us, event | category | flops | bytes accessed | tf_op | source)
XLA Modules:
  0.0 32.5 jit_solution(11742837238266154997)
XLA Ops:
  1.3 29.3 %shard_map.131 = (bf16[128,1024]{1,0:T(8,128)(2,1)}, bf16[128,1024]{1,0:T(8,128)(2,1)}, f32[128,128]{1,0:T(8,128)}) custom-call(bf16[128,1024]{1,0:T(8,128)(2,1)} %hk.1, bf16[128,1024]{1,0:T(8,128)(2,1)} %hv.1, bf16[128,1024]{1,0:T(8,128)(2,1)} %gate.1, bf16[1024,1024]{1,0:T(8,128)(2,1)} %taps.1, f32[1,1024]{1,0:T(1,128)} %bitcast.1, ...), custom_call_target="tpu_custom_call" | custom-call | tf_op jit(solution)/shard_map/pallas_call | solution.py:543
  30.6 1.8 %shard_map.132 = (bf16[128,1024]{1,0:T(8,128)(2,1)}, bf16[128,1024]{1,0:T(8,128)(2,1)}) custom-call(bf16[128,1024]{1,0:T(8,128)(2,1)} %get-tuple-element.5.h_rows, bf16[128,1024]{1,0:T(8,128)(2,1)} %get-tuple-element.6.attended, f32[128,128]{1,0:T(8,128)} %get-tuple-element.7.norm), custom_call_target="tpu_custom_call" | custom-call | tf_op jit(solution)/shard_map/pallas_call | solution.py:603
